TPU v7x, 32 devices: a whole 2x2x4 slice. The times are simulated.
32 devices in a mesh: gx: 4 (over y, x), gy: 8 (over z, core).
Axes of the slice: x: 2, y: 2, z: 4, core: 2. Of those that a mesh axis runs over, the one named last changes fastest.
Arguments:
- f_start: float32 [19, 4, 256, 512], P(None, None, 'gy', 'gx'), may hold values from 0.022 to 0.4, as said below
- cotangent: bfloat16 [19, 4, 256, 512], P(None, None, 'gy', 'gx'), may hold values from -6 to 6
- porosity: float32 [4, 8, 16], P('gx', 'gy'), may hold values from 0.1 to 0.9
- brick_ids: int32 [4, 8, 64], P('gx', 'gy'), may hold values from 0 to 127, as said below
- brick_slot: int32 [4, 8, 64], P('gx', 'gy'), may hold values from 0 to 15
Outputs:
- start_grad: float32 [19, 4, 256, 512], P(None, None, 'gy', 'gx')
- porosity_grad: float32 [4, 8, 16], P('gx', 'gy')
Inputs may be any that keep to these rules, and one draw needn't show every extreme that they name: `f_start`: each population is w_q times a factor between 0.8 and 1.2, w_q the weight of its direction. `brick_ids`: each device lists 64 distinct bricks of its own block; brick b covers layer b // 32, row b % 32 and all 128 cells along x of that block; device (0, 0) lists the last brick and device (0, 1) the first.
All inputs are finite; a program needn't handle non-finite values.
Results may differ from a plain program's by a relative error of at most 0.0003.
Values sent between devices are 32-bit elements; how exact they have to be, the bound alone decides.
A program may use at most 64 MiB of HBM per device.

v0:
```python
import jax
import jax.numpy as jnp
import numpy as np
from jax import lax
from jax.sharding import PartitionSpec as P

DIR_X = np.array([0, 1, -1, 0, 0, 0, 0, 1, -1, 1, -1, 1, -1, 1, -1, 0, 0, 0, 0])
DIR_Y = np.array([0, 0, 0, 1, -1, 0, 0, 1, 1, -1, -1, 0, 0, 0, 0, 1, -1, 1, -1])
DIR_Z = np.array([0, 0, 0, 0, 0, 1, -1, 0, 0, 0, 0, 1, 1, -1, -1, 1, 1, -1, -1])
WEIGHTS = np.array([1.0 / 3.0] + [1.0 / 18.0] * 6 + [1.0 / 36.0] * 12)
RELAX_RATE = 0.8


def extended(array, sides, width):
    for axis, dim in sides:
        devices, length = (lax.axis_size(axis), array.shape[dim])
        up = [(i, (i + 1) % devices) for i in range(devices)]
        down = [(j, i) for i, j in up]
        last = lax.slice_in_dim(array, length - width, length, axis=dim)
        leading = lax.slice_in_dim(array, 0, width, axis=dim)
        before = lax.ppermute(last, axis, up)
        after = lax.ppermute(leading, axis, down)
        array = jnp.concatenate([before, array, after], axis=dim)
    return array


def column(values):
    return np.asarray(values, np.float32)[:, None, None, None]


def collide(field, solid):
    density = jnp.sum(field, axis=0)
    inverse = (1.0 - solid) / density
    vel_x = jnp.sum(field * column(DIR_X), axis=0) * inverse
    vel_y = jnp.sum(field * column(DIR_Y), axis=0) * inverse
    vel_z = jnp.sum(field * column(DIR_Z), axis=0) * inverse
    along = column(DIR_X) * vel_x + column(DIR_Y) * vel_y + column(DIR_Z) * vel_z
    square = vel_x * vel_x + vel_y * vel_y + vel_z * vel_z
    balance = column(WEIGHTS) * density * (1.0 + 3.0 * along + 4.5 * along * along - 1.5 * square)
    return field - RELAX_RATE * (field - balance)


def pull(padded, sign):
    height = padded.shape[2] - 2
    width = padded.shape[3] - 2
    moved = []
    for lane in range(19):
        row_start = 1 - sign * int(DIR_Y[lane])
        col_start = 1 - sign * int(DIR_X[lane])
        piece = padded[lane, :, row_start : row_start + height, col_start : col_start + width]
        moved.append(jnp.roll(piece, sign * int(DIR_Z[lane]), axis=0))
    return jnp.stack(moved)


def extend(field):
    return extended(field, (("gx", 3), ("gy", 2)), 1)


def on_device(f_start, cotangent, porosity, brick_ids, brick_slot):
    layers_dev = f_start.shape[1]
    rows_dev = f_start.shape[2]
    cols_dev = f_start.shape[3]
    tile_count = cols_dev // 128
    brick_count = layers_dev * rows_dev * tile_count
    listed = brick_ids.reshape(-1)
    slots_of = brick_slot.reshape(-1)
    slot_table = porosity.reshape(-1)
    brick_hit = (listed[:, None] == jnp.arange(brick_count, dtype=jnp.int32)[None, :]).astype(
        jnp.float32
    )
    slot_hit = (
        slots_of[:, None] == jnp.arange(slot_table.shape[0], dtype=jnp.int32)[None, :]
    ).astype(jnp.float32)
    brick_value = jnp.sum(slot_hit * slot_table[None, :], axis=1)
    tile_value = jnp.sum(brick_hit * brick_value[:, None], axis=0)
    solid = jnp.broadcast_to(
        tile_value.reshape(layers_dev, rows_dev, tile_count, 1),
        (layers_dev, rows_dev, tile_count, 128),
    ).reshape(layers_dev, rows_dev, cols_dev)
    back_last = cotangent.astype(jnp.float32)
    after_one = pull(extend(collide(f_start, solid)), 1)
    back_two = pull(extend(back_last), -1)
    ignored, undo_two = jax.vjp(collide, after_one, solid)
    back_one, solid_bar_two = undo_two(back_two)
    back_one_pulled = pull(extend(back_one), -1)
    ignored_first, undo_one = jax.vjp(collide, f_start, solid)
    start_grad, solid_bar_one = undo_one(back_one_pulled)
    solid_bar = solid_bar_one + solid_bar_two
    tile_sums = jnp.sum(solid_bar.reshape(brick_count, 128), axis=1)
    brick_sum = jnp.sum(brick_hit * tile_sums[None, :], axis=1)
    slot_grad = jnp.sum(slot_hit * brick_sum[:, None], axis=0)
    return (start_grad, slot_grad.reshape(porosity.shape))


def solution(mesh):
    return jax.shard_map(
        on_device,
        mesh=mesh,
        in_specs=(
            P(None, None, "gy", "gx"),
            P(None, None, "gy", "gx"),
            P("gx", "gy", None),
            P("gx", "gy", None),
            P("gx", "gy", None),
        ),
        out_specs=(P(None, None, "gy", "gx"), P("gx", "gy", None)),
        check_vma=False,
    )
```

profile of v0, /device:TPU:0, one launch (start us, length us, event | category | flops | bytes accessed | tf_op | source)
XLA Modules:
  0.0 81.9 jit_solution(7936417145233469046)
XLA Ops:
  2.4 1.7 %multiply_reduce_fusion.12 = (f32[4,32,128]{2,1,0:T(8,128)S(1)}, f32[4,32,128]{2,1,0:T(8,128)S(1)}, f32[4,32,128]{2,1,0:T(8,128)S(1)}, f32[4,32,128]{2,1,0:T(8,128)S(1)}) fusion(f32[19,4,32,128]{3,2,1,0:T(8,128)} %param.26, f32[19]{0:T(128)} %constant.33, f32[19]{0:T(128)} %constant.34, f32[19]{0:T(128)} %constant.35), kind=kLoop, calls=%fused_computation.39 | loop fusion | flops 2113536 | bytes 1507556 | tf_op jit(solution)/shard_map/reduce_sum | solution.py:34
  6.1 1.5 %fusion.63 = (f32[19,4,32,1]{3,2,1,0:T(8,128)S(1)}, f32[19,4,32,1]{3,2,1,0:T(8,128)}) fusion(f32[19,4,32,128]{3,2,1,0:T(8,128)S(1)} %fusion.2), kind=kLoop, calls=%fused_computation.305 | loop fusion | bytes 38912 | tf_op jit(solution)/shard_map/slice | solution.py:20
  7.6 2.5 %copy.122 = f32[19,4,32,1]{2,1,3,0:T(4,128)} copy(f32[19,4,32,1]{3,2,1,0:T(8,128)} %get-tuple-element.131) | data formatting | bytes 19456 | tf_op jit(solution)/shard_map/slice | solution.py:19
  10.1 2.9 %collective-permute-start.4 = (f32[19,4,32,1]{2,1,3,0:T(4,128)}, f32[19,4,32,1]{2,1,3,0:T(4,128)}, u32[]{:S(2)}, u32[]{:S(2)}) collective-permute-start(f32[19,4,32,1]{2,1,3,0:T(4,128)} %copy.122), channel_id=1, source_target_pairs={{0,8},{8,16},{16,24},{24,0},{1,9},{9,17},{17,25},{25,1},{2,10},{10... | collective-permute-start | bytes 29192 | tf_op jit(solution)/shard_map/ppermute | solution.py:21
  15.1 1.4 %fusion.64 = (f32[19,4,32,1]{3,2,1,0:T(8,128)S(1)}, f32[19,4,32,1]{3,2,1,0:T(8,128)}) fusion(bf16[19,4,32,128]{3,2,1,0:T(8,128)(2,1)S(1)} %copy-done.7), kind=kLoop, calls=%fused_computation.306 | loop fusion | bytes 38912 | tf_op jit(solution)/shard_map/slice | solution.py:19
  16.5 2.4 %copy.116 = f32[19,4,32,1]{2,1,3,0:T(4,128)} copy(f32[19,4,32,1]{3,2,1,0:T(8,128)} %get-tuple-element.139) | data formatting | bytes 19456 | tf_op jit(solution)/shard_map/slice | solution.py:20
  18.9 2.0 %collective-permute-start = (f32[19,4,32,1]{2,1,3,0:T(4,128)}, f32[19,4,32,1]{2,1,3,0:T(4,128)}, u32[]{:S(2)}, u32[]{:S(2)}) collective-permute-start(f32[19,4,32,1]{2,1,3,0:T(4,128)} %copy.116), channel_id=1, source_target_pairs={{8,0},{16,8},{24,16},{0,24},{9,1},{17,9},{25,17},{1,25},{10,2},{18... | collective-permute-start | bytes 29192 | tf_op jit(solution)/shard_map/ppermute | solution.py:22
  23.5 2.3 %copy.123 = f32[19,4,32,1]{3,2,1,0:T(8,128)} copy(f32[19,4,32,1]{2,1,3,0:T(4,128)} %collective-permute-done.4) | data formatting | bytes 19456 | tf_op jit(solution)/shard_map/ppermute | solution.py:21
  25.8 2.4 %copy.125 = f32[19,4,32,1]{3,2,1,0:T(8,128)} copy(f32[19,4,32,1]{2,1,3,0:T(4,128)} %collective-permute-done.5) | data formatting | bytes 19456 | tf_op jit(solution)/shard_map/ppermute | solution.py:22
  30.6 2.4 %copy.117 = f32[19,4,32,1]{3,2,1,0:T(8,128)} copy(f32[19,4,32,1]{2,1,3,0:T(4,128)} %collective-permute-done) | data formatting | bytes 19456 | tf_op jit(solution)/shard_map/ppermute | solution.py:22
  32.9 2.3 %copy.119 = f32[19,4,32,1]{3,2,1,0:T(8,128)} copy(f32[19,4,32,1]{2,1,3,0:T(4,128)} %collective-permute-done.1) | data formatting | bytes 19456 | tf_op jit(solution)/shard_map/ppermute | solution.py:21
  35.3 2.0 %pad_maximum_fusion.6 = (f32[19,4,1,130]{3,2,1,0:T(1,128)S(1)}, f32[19,4,1,130]{3,2,1,0:T(1,128)S(1)}) fusion(f32[19,4,32,1]{3,2,1,0:T(8,128)} %copy.117, f32[19,4,32,128]{3,2,1,0:T(8,128)S(1)} %convert_element_type.2, f32[19,4,32,1]{3,2,1,0:T(8,128)} %copy.119), kind=kLoop, calls=%fused_computation.107 | loop fusion | flops 39520 | bytes 1343680 | tf_op jit(solution)/shard_map/concatenate | solution.py:23
  37.7 3.5 %collective-permute-start.7 = (f32[19,4,1,130]{3,2,1,0:T(1,128)S(1)}, f32[19,4,1,130]{3,2,1,0:T(1,128)S(1)}, u32[]{:S(2)}, u32[]{:S(2)}) collective-permute-start(f32[19,4,1,130]{3,2,1,0:T(1,128)S(1)} %get-tuple-element.90), channel_id=1, source_target_pairs={{1,0},{2,1},{3,2},{4,3},{5,4},{6,5},{7,6},{0,7},{9,8},{10,9},{11,1... | collective-permute-start | bytes 118568 | tf_op jit(solution)/shard_map/ppermute | solution.py:22
  46.6 3.2 %collective-permute-done.3 = f32[19,4,1,130]{3,2,1,0:T(1,128)S(1)} collective-permute-done((f32[19,4,1,130]{3,2,1,0:T(1,128)S(1)}, f32[19,4,1,130]{3,2,1,0:T(1,128)S(1)}, u32[]{:S(2)}, u32[]{:S(2)}) %collective-permute-start.3) | collective-permute-done | bytes 39552 | tf_op jit(solution)/shard_map/ppermute | solution.py:21
  51.1 1.3 %fusion.16 = (f32[4,32,128]{2,1,0:T(8,128)S(1)}, f32[4,32,128]{2,1,0:T(8,128)S(1)}, f32[4,32,128]{2,1,0:T(8,128)S(1)}, f32[4,32,128]{2,1,0:T(8,128)S(1)}, f32[4,32,128]{2,1,0:T(8,128)S(1)}) fusion(f32[19,4,32,128]{3,2,1,0:T(8,128)S(1)} %constant_dynamic-update-slice_fusion, f32[4,32,128]{2,1,0:T(8,128)S(1)} %bitcast.338, f32[19]{0:T(128)S(1)} %copy-done.22, ...), kind=kLoop, calls=%fused_computation.42 | loop fusion | flops 9879552 | bytes 1900848 | tf_op jit(solution)/shard_map/transpose(jvp())/reduce_sum | solution.py:39
  53.9 1.5 %fusion.62 = (f32[19,4,32,1]{3,2,1,0:T(8,128)S(1)}, f32[19,4,32,1]{3,2,1,0:T(8,128)}) fusion(f32[19,4,32,128]{3,2,1,0:T(8,128)S(1)} %add_add_fusion.1), kind=kLoop, calls=%fused_computation.304 | loop fusion | bytes 38912 | tf_op jit(solution)/shard_map/slice | solution.py:19
  55.4 1.8 %copy.128 = f32[19,4,32,1]{2,1,3,0:T(4,128)S(1)} copy(f32[19,4,32,1]{3,2,1,0:T(8,128)} %get-tuple-element.123) | data formatting | bytes 19456 | tf_op jit(solution)/shard_map/slice | solution.py:20
  57.2 2.9 %collective-permute-start.8 = (f32[19,4,32,1]{2,1,3,0:T(4,128)S(1)}, f32[19,4,32,1]{2,1,3,0:T(4,128)S(1)}, u32[]{:S(2)}, u32[]{:S(2)}) collective-permute-start(f32[19,4,32,1]{2,1,3,0:T(4,128)S(1)} %copy.128), channel_id=1, source_target_pairs={{8,0},{16,8},{24,16},{0,24},{9,1},{17,9},{25,17},{1,25},{10,2},{18... | collective-permute-start | bytes 29192 | tf_op jit(solution)/shard_map/ppermute | solution.py:22
  62.2 3.4 %collective-permute-done.9 = f32[19,4,32,1]{2,1,3,0:T(4,128)S(1)} collective-permute-done((f32[19,4,32,1]{2,1,3,0:T(4,128)S(1)}, f32[19,4,32,1]{2,1,3,0:T(4,128)S(1)}, u32[]{:S(2)}, u32[]{:S(2)}) %collective-permute-start.9) | collective-permute-done | bytes 9760 | tf_op jit(solution)/shard_map/ppermute | solution.py:21
  65.6 1.6 %copy.131 = f32[19,4,32,1]{3,2,1,0:T(8,128)} copy(f32[19,4,32,1]{2,1,3,0:T(4,128)S(1)} %collective-permute-done.9) | data formatting | bytes 19456 | tf_op jit(solution)/shard_map/ppermute | solution.py:21
  67.2 1.7 %pad_maximum_fusion = (f32[19,4,1,130]{3,2,1,0:T(1,128)S(1)}, f32[19,4,1,130]{3,2,1,0:T(1,128)S(1)}) fusion(f32[19,4,32,1]{3,2,1,0:T(8,128)S(1)} %copy.129, f32[19,4,32,128]{3,2,1,0:T(8,128)S(1)} %add_add_fusion.1, f32[19,4,32,1]{3,2,1,0:T(8,128)} %copy.131), kind=kLoop, calls=%fused_computation.101 | loop fusion | flops 39520 | bytes 1343680 | tf_op jit(solution)/shard_map/concatenate | solution.py:23
  71.9 3.0 %collective-permute-done.11 = f32[19,4,1,130]{3,2,1,0:T(1,128)S(1)} collective-permute-done((f32[19,4,1,130]{3,2,1,0:T(1,128)S(1)}, f32[19,4,1,130]{3,2,1,0:T(1,128)S(1)}, u32[]{:S(2)}, u32[]{:S(2)}) %collective-permute-start.11) | collective-permute-done | bytes 39552 | tf_op jit(solution)/shard_map/ppermute | solution.py:21
  76.5 1.3 %fusion.17 = (f32[4,32,128]{2,1,0:T(8,128)S(1)}, f32[4,32,128]{2,1,0:T(8,128)S(1)}, f32[4,32,128]{2,1,0:T(8,128)S(1)}, f32[4,32,128]{2,1,0:T(8,128)S(1)}, f32[4,32,128]{2,1,0:T(8,128)S(1)}) fusion(f32[19,4,32,128]{3,2,1,0:T(8,128)S(1)} %constant_dynamic-update-slice_fusion.38, f32[4,32,128]{2,1,0:T(8,128)S(1)} %get-tuple-element.19, f32[19]{0:T(128)S(1)} %copy-done.22, ...), kind=kLoop, calls=%fused_computation.43 | loop fusion | flops 9879552 | bytes 1900848 | tf_op jit(solution)/shard_map/transpose(jvp())/reduce_sum | solution.py:39
  79.0 2.8 %add_add_fusion = f32[19,4,32,128]{3,2,1,0:T(8,128)} fusion(f32[19,4,32,128]{3,2,1,0:T(8,128)} %copy-done.10, f32[4,32,128]{2,1,0:T(8,128)S(1)} %negate_add_fusion, f32[4,32,128]{2,1,0:T(8,128)S(1)} %get-tuple-element.144, f32[4,32,128]{2,1,0:T(8,128)S(1)} %get-tuple-element.143, f32[4,32,128]{2,1,0:T(8,128)S(1)} %get-tuple-element.142, ...), kind=kLoop, calls=%fused_computation.21 | loop fusion | flops 3112960 | bytes 2752740 | tf_op jit(solution)/shard_map/transpose(jvp())/add_any | solution.py:32
  (159 shorter events, 26.4 us)
Async XLA Ops:
  0.6 4.1 %copy-start.18 = (f32[19]{0:T(128)S(1)}, f32[19]{0:T(128)}, u32[]{:S(2)}) copy-start(f32[19]{0:T(128)} %constant.33) | copy-start | bytes 232
  0.6 4.1 %copy-start.19 = (f32[19]{0:T(128)S(1)}, f32[19]{0:T(128)}, u32[]{:S(2)}) copy-start(f32[19]{0:T(128)} %constant.34) | copy-start | bytes 232
  0.7 4.1 %copy-start.20 = (f32[19]{0:T(128)S(1)}, f32[19]{0:T(128)}, u32[]{:S(2)}) copy-start(f32[19]{0:T(128)} %constant.35) | copy-start | bytes 232
  0.7 4.1 %copy-start.21 = (f32[19]{0:T(128)S(1)}, f32[19]{0:T(128)}, u32[]{:S(2)}) copy-start(f32[19]{0:T(128)} %constant.32) | copy-start | bytes 232
  0.7 4.1 %copy-start.11 = (f32[19,4,32,128]{3,2,1,0:T(8,128)S(1)}, f32[19,4,32,128]{3,2,1,0:T(8,128)}, u32[]{:S(2)}) copy-start(f32[19,4,32,128]{3,2,1,0:T(8,128)} %param.26) | copy-start | bytes 3735556
  7.6 7.5 %copy-start.7 = (bf16[19,4,32,128]{3,2,1,0:T(8,128)(2,1)S(1)}, bf16[19,4,32,128]{3,2,1,0:T(8,128)(2,1)}, u32[]{:S(2)}) copy-start(bf16[19,4,32,128]{3,2,1,0:T(8,128)(2,1)} %param.27) | copy-start | bytes 1867780
  10.1 13.4 %collective-permute-start.4 = (f32[19,4,32,1]{2,1,3,0:T(4,128)}, f32[19,4,32,1]{2,1,3,0:T(4,128)}, u32[]{:S(2)}, u32[]{:S(2)}) collective-permute-start(f32[19,4,32,1]{2,1,3,0:T(4,128)} %copy.122), channel_id=1, source_target_pairs={{0,8},{8,16},{16,24},{24,0},{1,9},{9,17},{17,25},{25,1},{2,10},{10... | collective-permute-start | bytes 29192 | tf_op jit(solution)/shard_map/ppermute | solution.py:21
  14.1 11.7 %collective-permute-start.5 = (f32[19,4,32,1]{2,1,3,0:T(4,128)}, f32[19,4,32,1]{2,1,3,0:T(4,128)}, u32[]{:S(2)}, u32[]{:S(2)}) collective-permute-start(f32[19,4,32,1]{2,1,3,0:T(4,128)} %copy.124), channel_id=1, source_target_pairs={{8,0},{16,8},{24,16},{0,24},{9,1},{17,9},{25,17},{1,25},{10,2},{18... | collective-permute-start | bytes 29192 | tf_op jit(solution)/shard_map/ppermute | solution.py:22
  18.9 11.7 %collective-permute-start = (f32[19,4,32,1]{2,1,3,0:T(4,128)}, f32[19,4,32,1]{2,1,3,0:T(4,128)}, u32[]{:S(2)}, u32[]{:S(2)}) collective-permute-start(f32[19,4,32,1]{2,1,3,0:T(4,128)} %copy.116), channel_id=1, source_target_pairs={{8,0},{16,8},{24,16},{0,24},{9,1},{17,9},{25,17},{1,25},{10,2},{18... | collective-permute-start | bytes 29192 | tf_op jit(solution)/shard_map/ppermute | solution.py:22
  22.1 10.9 %collective-permute-start.1 = (f32[19,4,32,1]{2,1,3,0:T(4,128)}, f32[19,4,32,1]{2,1,3,0:T(4,128)}, u32[]{:S(2)}, u32[]{:S(2)}) collective-permute-start(f32[19,4,32,1]{2,1,3,0:T(4,128)} %copy.118), channel_id=1, source_target_pairs={{0,8},{8,16},{16,24},{24,0},{1,9},{9,17},{17,25},{25,1},{2,10},{10... | collective-permute-start | bytes 29192 | tf_op jit(solution)/shard_map/ppermute | solution.py:21
  35.3 2.1 %copy-start.1 = (f32[19,4,32,1]{3,2,1,0:T(8,128)S(1)}, f32[19,4,32,1]{3,2,1,0:T(8,128)}, u32[]{:S(2)}) copy-start(f32[19,4,32,1]{3,2,1,0:T(8,128)} %copy.119) | copy-start | bytes 29188
  37.5 3.7 %copy-start.3 = (f32[19,4,32,1]{3,2,1,0:T(8,128)S(1)}, f32[19,4,32,1]{3,2,1,0:T(8,128)}, u32[]{:S(2)}) copy-start(f32[19,4,32,1]{3,2,1,0:T(8,128)} %copy.123) | copy-start | bytes 29188
  37.5 3.7 %copy-start.12 = (f32[19,4,32,128]{3,2,1,0:T(8,128)S(1)}, f32[19,4,32,128]{3,2,1,0:T(8,128)}, u32[]{:S(2)}) copy-start(f32[19,4,32,128]{3,2,1,0:T(8,128)} %constant_dynamic-update-slice_fusion.37) | copy-start | bytes 3735556
  37.6 6.5 %collective-permute-start.6 = (f32[19,4,1,130]{3,2,1,0:T(1,128)S(1)}, f32[19,4,1,130]{3,2,1,0:T(1,128)S(1)}, u32[]{:S(2)}, u32[]{:S(2)}) collective-permute-start(f32[19,4,1,130]{3,2,1,0:T(1,128)S(1)} %get-tuple-element.91), channel_id=1, source_target_pairs={{0,1},{1,2},{2,3},{3,4},{4,5},{5,6},{6,7},{7,0},{8,9},{9,10},{10,1... | collective-permute-start | bytes 118568 | tf_op jit(solution)/shard_map/ppermute | solution.py:21
  37.7 3.6 %copy-start.5 = (f32[19,4,32,1]{3,2,1,0:T(8,128)S(1)}, f32[19,4,32,1]{3,2,1,0:T(8,128)}, u32[]{:S(2)}) copy-start(f32[19,4,32,1]{3,2,1,0:T(8,128)} %copy.125) | copy-start | bytes 29188
  37.7 6.5 %collective-permute-start.7 = (f32[19,4,1,130]{3,2,1,0:T(1,128)S(1)}, f32[19,4,1,130]{3,2,1,0:T(1,128)S(1)}, u32[]{:S(2)}, u32[]{:S(2)}) collective-permute-start(f32[19,4,1,130]{3,2,1,0:T(1,128)S(1)} %get-tuple-element.90), channel_id=1, source_target_pairs={{1,0},{2,1},{3,2},{4,3},{5,4},{6,5},{7,6},{0,7},{9,8},{10,9},{11,1... | collective-permute-start | bytes 118568 | tf_op jit(solution)/shard_map/ppermute | solution.py:22
  42.8 3.7 %collective-permute-start.2 = (f32[19,4,1,130]{3,2,1,0:T(1,128)S(1)}, f32[19,4,1,130]{3,2,1,0:T(1,128)S(1)}, u32[]{:S(2)}, u32[]{:S(2)}) collective-permute-start(f32[19,4,1,130]{3,2,1,0:T(1,128)S(1)} %get-tuple-element.97), channel_id=1, source_target_pairs={{1,0},{2,1},{3,2},{4,3},{5,4},{6,5},{7,6},{0,7},{9,8},{10,9},{11,1... | collective-permute-start | bytes 118568 | tf_op jit(solution)/shard_map/ppermute | solution.py:22
  44.1 5.6 %collective-permute-start.3 = (f32[19,4,1,130]{3,2,1,0:T(1,128)S(1)}, f32[19,4,1,130]{3,2,1,0:T(1,128)S(1)}, u32[]{:S(2)}, u32[]{:S(2)}) collective-permute-start(f32[19,4,1,130]{3,2,1,0:T(1,128)S(1)} %get-tuple-element.96), channel_id=1, source_target_pairs={{0,1},{1,2},{2,3},{3,4},{4,5},{5,6},{6,7},{7,0},{8,9},{9,10},{10,1... | collective-permute-start | bytes 118568 | tf_op jit(solution)/shard_map/ppermute | solution.py:21
  57.2 4.5 %collective-permute-start.8 = (f32[19,4,32,1]{2,1,3,0:T(4,128)S(1)}, f32[19,4,32,1]{2,1,3,0:T(4,128)S(1)}, u32[]{:S(2)}, u32[]{:S(2)}) collective-permute-start(f32[19,4,32,1]{2,1,3,0:T(4,128)S(1)} %copy.128), channel_id=1, source_target_pairs={{8,0},{16,8},{24,16},{0,24},{9,1},{17,9},{25,17},{1,25},{10,2},{18... | collective-permute-start | bytes 29192 | tf_op jit(solution)/shard_map/ppermute | solution.py:22
  60.5 5.1 %collective-permute-start.9 = (f32[19,4,32,1]{2,1,3,0:T(4,128)S(1)}, f32[19,4,32,1]{2,1,3,0:T(4,128)S(1)}, u32[]{:S(2)}, u32[]{:S(2)}) collective-permute-start(f32[19,4,32,1]{2,1,3,0:T(4,128)S(1)} %copy.130), channel_id=1, source_target_pairs={{0,8},{8,16},{16,24},{24,0},{1,9},{9,17},{17,25},{25,1},{2,10},{10... | collective-permute-start | bytes 29192 | tf_op jit(solution)/shard_map/ppermute | solution.py:21
  69.2 2.6 %collective-permute-start.10 = (f32[19,4,1,130]{3,2,1,0:T(1,128)S(1)}, f32[19,4,1,130]{3,2,1,0:T(1,128)S(1)}, u32[]{:S(2)}, u32[]{:S(2)}) collective-permute-start(f32[19,4,1,130]{3,2,1,0:T(1,128)S(1)} %get-tuple-element.85), channel_id=1, source_target_pairs={{1,0},{2,1},{3,2},{4,3},{5,4},{6,5},{7,6},{0,7},{9,8},{10,9},{11,1... | collective-permute-start | bytes 118568 | tf_op jit(solution)/shard_map/ppermute | solution.py:22
  69.2 5.7 %collective-permute-start.11 = (f32[19,4,1,130]{3,2,1,0:T(1,128)S(1)}, f32[19,4,1,130]{3,2,1,0:T(1,128)S(1)}, u32[]{:S(2)}, u32[]{:S(2)}) collective-permute-start(f32[19,4,1,130]{3,2,1,0:T(1,128)S(1)} %get-tuple-element.84), channel_id=1, source_target_pairs={{0,1},{1,2},{2,3},{3,4},{4,5},{5,6},{6,7},{7,0},{8,9},{9,10},{10,1... | collective-permute-start | bytes 118568 | tf_op jit(solution)/shard_map/ppermute | solution.py:21
  75.8 2.0 %copy-start.14 = (f32[4,32,128]{2,1,0:T(8,128)S(1)}, f32[4,32,128]{2,1,0:T(8,128)}, u32[]{:S(2)}) copy-start(f32[4,32,128]{2,1,0:T(8,128)} %copy-done.13) | copy-start | bytes 196612
  75.8 2.0 %copy-start.17 = (f32[4,32,128]{2,1,0:T(8,128)S(1)}, f32[4,32,128]{2,1,0:T(8,128)}, u32[]{:S(2)}) copy-start(f32[4,32,128]{2,1,0:T(8,128)} %get-tuple-element.32) | copy-start | bytes 196612
  (13 other events, 18.4 us)
where the time goes:
time: 82.6 us; the launch traced here: 81.9 us
  local copies, waits for them, and re-layouts  31.5 us (38%)
  other arithmetic  22.6 us (27%)
  starting transfers between devices  14.5 us (18%)
  waiting for transfers between devices  11.8 us (14%)
  between operations  1.48 us (2%)
    ppermute x6, starting transfers between devices, extended(): after = lax.ppermute(leading, axis, down)  10.8 us
    ppermute x6, waiting for transfers between devices, extended(): before = lax.ppermute(last, axis, up)  9.63 us
    slice x5, local copies, waits for them, and re-layouts, extended(): last = lax.slice_in_dim(array, length - width, length, axis=dim)  7 us
    slice x4, local copies, waits for them, and re-layouts, extended(): leading = lax.slice_in_dim(array, 0, width, axis=dim)  6.84 us
    ppermute x3, local copies, waits for them, and re-layouts, extended(): before = lax.ppermute(last, axis, up)  6.26 us
    unnamed x53, local copies, waits for them, and re-layouts  6.01 us
    ppermute x3, local copies, waits for them, and re-layouts, extended(): after = lax.ppermute(leading, axis, down)  5.24 us
    concatenate x3, other arithmetic, extended(): array = jnp.concatenate([before, array, after], axis=dim)  4.22 us
  transfers between devices with their start and end apart: 12, of which 6 were waited for; matrix products, arithmetic and copies ran while one was open for 25% of the time, Pallas kernels for 0%

commit v1 on v0

v1 whole, which is shorter than its diff:
```python
import functools

import jax
import jax.numpy as jnp
from jax import lax
from jax.experimental import pallas as pl
from jax.experimental.pallas import tpu as pltpu
from jax.sharding import PartitionSpec as P

EX = (0, 1, -1, 0, 0, 0, 0, 1, -1, 1, -1, 1, -1, 1, -1, 0, 0, 0, 0)
EY = (0, 0, 0, 1, -1, 0, 0, 1, 1, -1, -1, 0, 0, 0, 0, 1, -1, 1, -1)
EZ = (0, 0, 0, 0, 0, 1, -1, 0, 0, 0, 0, 1, 1, -1, -1, 1, 1, -1, -1)
Q = 19
PAIRS = ((1, 2), (3, 4), (5, 6), (7, 10), (9, 8), (11, 14), (13, 12), (15, 18), (17, 16))
AXIS_W = 1.0 / 18.0
EDGE_W = 1.0 / 36.0
MESH = pl.DeviceIdType.MESH


def rank_among(q, component):
    return [p for p in range(Q) if component[p] == component[q]].index(q)


def side(step):
    return 0 if step > 0 else 1


def moments(d):
    return (
        (d[0], d[3] + d[4] + d[5] + d[6]),
        (d[1], (d[3] - d[4]) + (d[7] + d[8])),
        (d[2], (d[5] - d[6]) + (d[7] - d[8])),
    )


def along(vec):
    x, y, z = vec
    return (x, y, z, x + y, x - y, x + z, x - z, y + z, y - z)


def density_velocity(f, s):
    rho = f[0]
    diffs = []
    for a, b in PAIRS:
        rho = rho + (f[a] + f[b])
        diffs.append(f[a] - f[b])
    m = [a + b for a, b in moments(diffs)]
    inverse = s / rho
    return rho, m, [c * inverse for c in m]


def collide(f, rho, v):
    square = v[0] * v[0] + v[1] * v[1] + v[2] * v[2]
    base = 1.0 - 1.5 * square
    out = [None] * Q
    rho_axis = (0.8 * AXIS_W) * rho
    rho_edge = (0.8 * EDGE_W) * rho
    out[0] = 0.2 * f[0] + (0.8 / 3.0) * rho * base
    for n, ((a, b), c) in enumerate(zip(PAIRS, along(v))):
        scale = rho_axis if n < 3 else rho_edge
        even = scale * (base + 4.5 * c * c)
        odd = scale * (3.0 * c)
        out[a] = 0.2 * f[a] + (even + odd)
        out[b] = 0.2 * f[b] + (even - odd)
    return out


def collide_back(g, m, v, s):
    p = [g[a] + g[b] for a, b in PAIRS]
    d = [g[a] - g[b] for a, b in PAIRS]
    g1 = [AXIS_W * a + EDGE_W * b for a, b in moments(d)]
    xy, xz, yz = p[3] + p[4], p[5] + p[6], p[7] + p[8]
    g0 = (1.0 / 3.0) * g[0] + AXIS_W * (p[0] + p[1] + p[2]) + EDGE_W * (xy + xz + yz)
    gxx = AXIS_W * p[0] + EDGE_W * (xy + xz)
    gyy = AXIS_W * p[1] + EDGE_W * (xy + yz)
    gzz = AXIS_W * p[2] + EDGE_W * (xz + yz)
    gxy = EDGE_W * (p[3] - p[4])
    gxz = EDGE_W * (p[5] - p[6])
    gyz = EDGE_W * (p[7] - p[8])
    h = (
        gxx * v[0] + gxy * v[1] + gxz * v[2],
        gxy * v[0] + gyy * v[1] + gyz * v[2],
        gxz * v[0] + gyz * v[1] + gzz * v[2],
    )
    square = v[0] * v[0] + v[1] * v[1] + v[2] * v[2]
    b = [3.0 * g1[i] + 9.0 * h[i] - 3.0 * (g0 * v[i]) for i in range(3)]
    rest = g0 * (1.0 + 1.5 * square) - 4.5 * (v[0] * h[0] + v[1] * h[1] + v[2] * h[2])
    base = 0.8 * rest
    scale = 0.8 * s
    out = [None] * Q
    out[0] = 0.2 * g[0] + base
    for (a, o), c in zip(PAIRS, along([scale * c for c in b])):
        out[a] = 0.2 * g[a] + (base + c)
        out[o] = 0.2 * g[o] + (base - c)
    solid_bar = -0.8 * (b[0] * m[0] + b[1] * m[1] + b[2] * m[2])
    return out, solid_bar


def kernel(
    f_ref, cot_ref, por_ref, ids_ref, slot_ref, grad_ref, pgrad_ref,
    s_ref, v_ref, m_ref, sb_ref, a_ref, b_ref, c_ref,
    xs1, xr1, ys1, yr1, cs1, cr1, xs2, xr2, ys2, yr2, cs2, cr2, send_sem, recv_sem,
):
    layers, rows, cols = f_ref.shape[1:]
    n_x, n_y = lax.axis_size("gx"), lax.axis_size("gy")
    my_x, my_y = lax.axis_index("gx"), lax.axis_index("gy")

    def device(dx, dy):
        return (lax.rem(my_x + dx + n_x, n_x), lax.rem(my_y + dy + n_y, n_y))

    straight = ((1, 0), (-1, 0), (0, 1), (0, -1))
    corners = ((1, 1), (1, -1), (-1, 1), (-1, -1))
    barrier = pltpu.get_barrier_semaphore()
    for dx, dy in straight + corners:
        pl.semaphore_signal(barrier, inc=1, device_id=device(dx, dy), device_id_type=MESH)

    lane = lax.broadcasted_iota(jnp.int32, (rows, cols), 1)
    row = lax.broadcasted_iota(jnp.int32, (rows, cols), 0)
    lane1 = lax.broadcasted_iota(jnp.int32, (1, cols), 1)

    def copies(phase, xs, xr, ys, yr, cs, cr):
        out = []
        for n, (dx, dy) in enumerate(straight + corners):
            if n < 2:
                src, dst = xs.at[n], xr.at[n]
            elif n < 4:
                src, dst = ys.at[n - 2], yr.at[n - 2]
            else:
                src, dst = cs.at[n - 4], cr.at[n - 4]
            out.append(
                pltpu.make_async_remote_copy(
                    src_ref=src, dst_ref=dst,
                    send_sem=send_sem.at[phase, n], recv_sem=recv_sem.at[phase, n],
                    device_id=device(dx, dy), device_id_type=MESH,
                )
            )
        return out

    def pack(parts, xs, ys, cs):
        def layer(z, carry):
            carry = list(carry)
            for kind, (read, sign) in enumerate(parts):
                for q in range(Q):
                    dx, dy = sign * EX[q], sign * EY[q]
                    if not dx and not dy:
                        continue
                    plane = read(q, z)
                    if dx:
                        j = kind * 5 * layers + rank_among(q, EX) * layers + z
                        start = cols - 1 if dx > 0 else 0
                        moved = pltpu.roll(plane, lax.rem(j - start + cols, cols), 1)
                        carry[side(dx)] = jnp.where(lane == j, moved, carry[side(dx)])
                    if dy:
                        jy = kind * 5 * layers + rank_among(q, EY) * layers + z
                        edge = plane[rows - 8 :] if dy > 0 else plane[:8]
                        if dx:
                            edge = pltpu.roll(edge, dx % cols, 1)
                        edge = edge[7:8] if dy > 0 else edge[0:1]
                        ys[side(dy), pl.ds(jy, 1), :] = edge
                        if dx:
                            cs[2 * side(dx) + side(dy), pl.ds(kind * layers + z, 1), :] = edge
            return tuple(carry)

        zero = jnp.zeros((rows, cols), jnp.float32)
        ends = lax.fori_loop(0, layers, layer, (zero, zero))
        xs[0] = ends[0]
        xs[1] = ends[1]

    def stream(read, sign, kind, xr, yr, cr, write):
        def layer(z, carry):
            for q in range(Q):
                dx, dy, dz = sign * EX[q], sign * EY[q], sign * EZ[q]
                from_z = lax.rem(z - dz + layers, layers) if dz else z
                plane = read(q, from_z)
                end = 0 if dx > 0 else cols - 1
                if dx:
                    plane = pltpu.roll(plane, dx % cols, 1)
                    j = kind * 5 * layers + rank_among(q, EX) * layers + from_z
                    column = pltpu.roll(xr[side(dx)], lax.rem(end - j + cols, cols), 1)
                    plane = jnp.where(lane == end, column, plane)
                if dy:
                    plane = pltpu.roll(plane, dy % rows, 0)
                    jy = kind * 5 * layers + rank_among(q, EY) * layers + from_z
                    edge = yr[side(dy), pl.ds(jy, 1), :]
                    if dx:
                        corner = cr[2 * side(dx) + side(dy), pl.ds(kind * layers + from_z, 1), :]
                        edge = jnp.where(lane1 == end, corner, edge)
                    plane = jnp.where(row == (0 if dy > 0 else rows - 1), edge, plane)
                write(q, z, plane)
            return carry

        lax.fori_loop(0, layers, layer, 0)

    bricks = layers * rows
    ids = ids_ref[0]
    slots = slot_ref[0]
    listed = ids.shape[1]
    value = jnp.zeros((1, listed), jnp.float32)
    for k in range(por_ref.shape[2]):
        value = jnp.where(slots == k, por_ref[0, 0, k], value)
    brick_of_row = lax.broadcasted_iota(jnp.int32, (bricks, listed), 0)
    hit = brick_of_row == ids
    solid = jnp.sum(jnp.where(hit, value, 0.0), axis=1, keepdims=True)
    s_ref[...] = jnp.broadcast_to(1.0 - solid, (bricks, cols)).reshape(layers, rows, cols)

    chunks = rows // 8

    def each_chunk(body):
        def step(i, carry):
            z = lax.div(i, chunks)
            r = pl.multiple_of(lax.rem(i, chunks) * 8, 8)
            body(z, pl.ds(r, 8))
            return carry

        lax.fori_loop(0, layers * chunks, step, 0)

    def first_collision(z, r):
        f = [f_ref[q, z, r, :] for q in range(Q)]
        rho, m, v = density_velocity(f, s_ref[z, r, :])
        for i in range(3):
            v_ref[i, z, r, :] = v[i]
            m_ref[i, z, r, :] = m[i]
        for q, value in enumerate(collide(f, rho, v)):
            c_ref[q, z, r, :] = value

    each_chunk(first_collision)

    def read_c(q, z):
        return c_ref[q, z]

    def read_cot(q, z):
        return cot_ref[q, z].astype(jnp.float32)

    pack(((read_c, 1), (read_cot, -1)), xs1, ys1, cs1)
    pl.semaphore_wait(barrier, len(straight + corners))
    first = copies(0, xs1, xr1, ys1, yr1, cs1, cr1)
    for copy in first:
        copy.start()
    for copy in first:
        copy.wait()

    def write_a(q, z, plane):
        a_ref[q, z] = plane

    def write_b(q, z, plane):
        b_ref[q, z] = plane

    stream(read_c, 1, 0, xr1, yr1, cr1, write_a)
    stream(read_cot, -1, 1, xr1, yr1, cr1, write_b)

    def second_back(z, r):
        s = s_ref[z, r, :]
        rho, m, v = density_velocity([a_ref[q, z, r, :] for q in range(Q)], s)
        back, bar = collide_back([b_ref[q, z, r, :] for q in range(Q)], m, v, s)
        sb_ref[z, r, :] = bar
        for q, value in enumerate(back):
            c_ref[q, z, r, :] = value

    each_chunk(second_back)

    pack(((read_c, -1),), xs2, ys2, cs2)
    second = copies(1, xs2, xr2, ys2, yr2, cs2, cr2)
    for copy in second:
        copy.start()
    for copy in second:
        copy.wait()
    stream(read_c, -1, 0, xr2, yr2, cr2, write_a)

    def first_back(z, r):
        v = [v_ref[i, z, r, :] for i in range(3)]
        m = [m_ref[i, z, r, :] for i in range(3)]
        back, bar = collide_back([a_ref[q, z, r, :] for q in range(Q)], m, v, s_ref[z, r, :])
        sb_ref[z, r, :] = sb_ref[z, r, :] + bar
        for q, value in enumerate(back):
            grad_ref[q, z, r, :] = value

    each_chunk(first_back)

    sums = jnp.sum(sb_ref[...].reshape(bricks, cols), axis=1, keepdims=True)
    brick_sum = jnp.sum(jnp.where(hit, sums, 0.0), axis=0, keepdims=True)
    table = por_ref.shape[2]
    slot_of_row = lax.broadcasted_iota(jnp.int32, (table, listed), 0)
    slot_sum = jnp.sum(jnp.where(slot_of_row == slots, brick_sum, 0.0), axis=1, keepdims=True)
    diagonal = lax.broadcasted_iota(jnp.int32, (table, table), 0) == lax.broadcasted_iota(
        jnp.int32, (table, table), 1
    )
    pgrad_ref[0] = jnp.sum(jnp.where(diagonal, slot_sum, 0.0), axis=0, keepdims=True)


def on_device(f_start, cotangent, porosity, brick_ids, brick_slot):
    _, layers, rows, cols = f_start.shape
    vmem = pl.BlockSpec(memory_space=pltpu.VMEM)
    field = pltpu.VMEM((Q, layers, rows, cols), jnp.float32)
    vector = pltpu.VMEM((3, layers, rows, cols), jnp.float32)
    scalar = pltpu.VMEM((layers, rows, cols), jnp.float32)

    def up8(count):
        return -(-count // 8) * 8

    halos = []
    for kinds in (2, 1):
        x = pltpu.VMEM((2, rows, cols), jnp.float32)
        y = pltpu.VMEM((2, up8(kinds * 5 * layers), cols), jnp.float32)
        c = pltpu.VMEM((4, up8(kinds * layers), cols), jnp.float32)
        halos += [x, x, y, y, c, c]
    return pl.pallas_call(
        kernel,
        out_shape=(
            jax.ShapeDtypeStruct(f_start.shape, jnp.float32),
            jax.ShapeDtypeStruct(porosity.shape, jnp.float32),
        ),
        in_specs=[vmem, vmem, pl.BlockSpec(memory_space=pltpu.SMEM), vmem, vmem],
        out_specs=(vmem, vmem),
        scratch_shapes=[scalar, vector, vector, scalar, field, field, field]
        + halos
        + [pltpu.SemaphoreType.DMA((2, 8)), pltpu.SemaphoreType.DMA((2, 8))],
        compiler_params=pltpu.CompilerParams(
            collective_id=0, has_side_effects=True, vmem_limit_bytes=40 * 1024 * 1024
        ),
    )(f_start, cotangent, porosity, brick_ids, brick_slot)


def solution(mesh):
    field = P(None, None, "gy", "gx")
    table = P("gx", "gy", None)
    return jax.shard_map(
        on_device,
        mesh=mesh,
        in_specs=(field, field, table, table, table),
        out_specs=(field, table),
        check_vma=False,
    )
```

time: 82.6 us -> 26.1 us (0.32)
  local copies, waits for them, and re-layouts: 31.5 us -> 5.87 us
  other arithmetic: 22.6 us -> 0 us
  Pallas kernels: 0 us -> 19.4 us
  starting transfers between devices: 14.5 us -> 0 us
  waiting for transfers between devices: 11.8 us -> 0 us
  between operations: 1.48 us -> 0.65 us
    pallas_call x0 -> x1, Pallas kernels: none -> 19.4 us  [on_device(): pl.pallas_call(kernel, out_shape=(jax.ShapeDtypeStruct(f_start.shape, jnp...]
    ppermute x12 -> x0, starting transfers between devices: 14.5 us -> none  [the longest x6 10.8 us: extended(): after = lax.ppermute(leading, axis, down)]
    slice x9 -> x0, local copies, waits for them, and re-layouts: 13.8 us -> none  [the longest x5 7 us: extended(): last = lax.slice_in_dim(array, length - width, length, axis=dim)]
    ppermute x12 -> x0, waiting for transfers between devices: 11.8 us -> none  [the longest x6 9.63 us: extended(): before = lax.ppermute(last, axis, up)]
    ppermute x6 -> x0, local copies, waits for them, and re-layouts: 11.5 us -> none  [the longest x3 6.26 us: extended(): before = lax.ppermute(last, axis, up)]
    reduce_sum x9 -> x0, other arithmetic: 7.34 us -> none  [the longest x2 2.67 us: collide(): 1.0 + 3.0 * along + 4.5 * along * along - 1.5 * square]
    concatenate x3 -> x0, other arithmetic: 4.22 us -> none  [extended(): array = jnp.concatenate([before, array, after], axis=dim)]
    add_any x4 -> x0, other arithmetic: 4.19 us -> none  [the longest x2 3.36 us: collide(): density = jnp.sum(field, axis=0)]
  transfers between devices with their start and end apart: 12 -> 0, of which waited for: 6 -> 0; matrix products, arithmetic and copies ran while one was open for 25% -> 0% of each run, Pallas kernels for 0% -> 0%
where the time goes in v1:
time: 26.1 us; the launch traced here: 25.9 us
  Pallas kernels  19.4 us (74%)
  local copies, waits for them, and re-layouts  5.87 us (22%)
  between operations  0.65 us (2%)
    pallas_call x1, Pallas kernels, on_device(): pl.pallas_call(kernel, out_shape=(jax.ShapeDtypeStruct(f_start.shape, jnp...  19.4 us
    unnamed x12, local copies, waits for them, and re-layouts  5.87 us

profile of v1, /device:TPU:0, one launch (start us, length us, event | category | flops | bytes accessed | tf_op | source)
XLA Modules:
  0.0 25.9 jit_solution(1478518401100527942)
XLA Ops:
  0.6 0.0 copy-start
  0.6 1.3 %copy-done = f32[19,4,32,128]{3,2,1,0:T(8,128)S(1)} copy-done((f32[19,4,32,128]{3,2,1,0:T(8,128)S(1)}, f32[19,4,32,128]{3,2,1,0:T(8,128)}, u32[]{:S(2)}) %copy-start) | copy-done | bytes 1245208
  1.9 0.0 copy-start.1
  1.9 1.1 %copy-done.1 = bf16[19,4,32,128]{3,2,1,0:T(8,128)(2,1)S(1)} copy-done((bf16[19,4,32,128]{3,2,1,0:T(8,128)(2,1)S(1)}, bf16[19,4,32,128]{3,2,1,0:T(8,128)(2,1)}, u32[]{:S(2)}) %copy-start.1) | copy-done | bytes 622616
  3.0 0.0 copy-start.2
  3.0 0.7 %copy-done.2 = f32[1,1,16]{2,1,0:T(1,128)S(1)} copy-done((f32[1,1,16]{2,1,0:T(1,128)S(1)}, f32[1,1,16]{2,1,0:T(1,128)}, u32[]{:S(2)}) %copy-start.2) | copy-done | bytes 88
  3.7 0.0 copy-start.3
  3.7 0.7 %copy-done.3 = s32[1,1,64]{2,1,0:T(1,128)S(1)} copy-done((s32[1,1,64]{2,1,0:T(1,128)S(1)}, s32[1,1,64]{2,1,0:T(1,128)}, u32[]{:S(2)}) %copy-start.3) | copy-done | bytes 280
  4.3 0.0 copy-start.4
  4.3 0.7 %copy-done.4 = s32[1,1,64]{2,1,0:T(1,128)S(1)} copy-done((s32[1,1,64]{2,1,0:T(1,128)S(1)}, s32[1,1,64]{2,1,0:T(1,128)}, u32[]{:S(2)}) %copy-start.4) | copy-done | bytes 280
  5.0 19.4 %shard_map.68 = (f32[19,4,32,128]{3,2,1,0:T(8,128)S(1)}, f32[1,1,16]{2,1,0:T(1,128)S(1)}) custom-call(f32[19,4,32,128]{3,2,1,0:T(8,128)S(1)} %copy-done, bf16[19,4,32,128]{3,2,1,0:T(8,128)(2,1)S(1)} %copy-done.1, f32[1,1,16]{2,1,0:T(1,128)S(1)} %copy-done.2, s32[1,1,64]{2,1,0:T(1,128)S(1)} %copy-done.3, s32[1,1,64]{2,1,0:T(1,128)S(1)} %copy-done.4), custom_call_target="tpu_custom_call" | custom-call | tf_op jit(solution)/shard_map/pallas_call | solution.py:306
  24.4 1.0 %copy.9 = f32[19,4,32,128]{3,2,1,0:T(8,128)} copy(f32[19,4,32,128]{3,2,1,0:T(8,128)S(1)} %get-tuple-element.4) | data formatting | bytes 2490368
  25.4 0.5 %copy.10 = f32[1,1,16]{2,1,0:T(1,128)} copy(f32[1,1,16]{2,1,0:T(1,128)S(1)} %get-tuple-element.5) | data formatting | bytes 128
Async XLA Ops:
  0.6 1.3 %copy-start = (f32[19,4,32,128]{3,2,1,0:T(8,128)S(1)}, f32[19,4,32,128]{3,2,1,0:T(8,128)}, u32[]{:S(2)}) copy-start(f32[19,4,32,128]{3,2,1,0:T(8,128)} %f_ref.1) | copy-start | bytes 3735556
  1.9 1.1 %copy-start.1 = (bf16[19,4,32,128]{3,2,1,0:T(8,128)(2,1)S(1)}, bf16[19,4,32,128]{3,2,1,0:T(8,128)(2,1)}, u32[]{:S(2)}) copy-start(bf16[19,4,32,128]{3,2,1,0:T(8,128)(2,1)} %cot_ref.1) | copy-start | bytes 1867780
  3.0 0.7 %copy-start.2 = (f32[1,1,16]{2,1,0:T(1,128)S(1)}, f32[1,1,16]{2,1,0:T(1,128)}, u32[]{:S(2)}) copy-start(f32[1,1,16]{2,1,0:T(1,128)} %por_ref.1) | copy-start | bytes 196
  3.7 0.7 %copy-start.3 = (s32[1,1,64]{2,1,0:T(1,128)S(1)}, s32[1,1,64]{2,1,0:T(1,128)}, u32[]{:S(2)}) copy-start(s32[1,1,64]{2,1,0:T(1,128)} %ids_ref.1) | copy-start | bytes 772
  4.3 0.7 %copy-start.4 = (s32[1,1,64]{2,1,0:T(1,128)S(1)}, s32[1,1,64]{2,1,0:T(1,128)}, u32[]{:S(2)}) copy-start(s32[1,1,64]{2,1,0:T(1,128)} %slot_ref.1) | copy-start | bytes 772

commit v2 on v1

v2 whole, which is shorter than its diff:
```python
import jax
import jax.numpy as jnp
from jax import lax
from jax.experimental import pallas as pl
from jax.experimental.pallas import tpu as pltpu
from jax.sharding import PartitionSpec as P

EX = (0, 1, -1, 0, 0, 0, 0, 1, -1, 1, -1, 1, -1, 1, -1, 0, 0, 0, 0)
EY = (0, 0, 0, 1, -1, 0, 0, 1, 1, -1, -1, 0, 0, 0, 0, 1, -1, 1, -1)
EZ = (0, 0, 0, 0, 0, 1, -1, 0, 0, 0, 0, 1, 1, -1, -1, 1, 1, -1, -1)
Q = 19
PAIRS = ((1, 2), (3, 4), (5, 6), (7, 10), (9, 8), (11, 14), (13, 12), (15, 18), (17, 16))
AXIS_W = 1.0 / 18.0
EDGE_W = 1.0 / 36.0
MESH = pl.DeviceIdType.MESH


def rank_among(q, component):
    return [p for p in range(Q) if component[p] == component[q]].index(q)


def side(step):
    return 0 if step > 0 else 1


def moments(d):
    return (
        (d[0], d[3] + d[4] + d[5] + d[6]),
        (d[1], (d[3] - d[4]) + (d[7] + d[8])),
        (d[2], (d[5] - d[6]) + (d[7] - d[8])),
    )


def along(vec):
    x, y, z = vec
    return (x, y, z, x + y, x - y, x + z, x - z, y + z, y - z)


def density_velocity(f, s):
    rho = f[0]
    diffs = []
    for a, b in PAIRS:
        rho = rho + (f[a] + f[b])
        diffs.append(f[a] - f[b])
    m = [a + b for a, b in moments(diffs)]
    inverse = s / rho
    return rho, m, [c * inverse for c in m]


def collide(f, rho, v):
    square = v[0] * v[0] + v[1] * v[1] + v[2] * v[2]
    base = 1.0 - 1.5 * square
    out = [None] * Q
    rho_axis = (0.8 * AXIS_W) * rho
    rho_edge = (0.8 * EDGE_W) * rho
    out[0] = 0.2 * f[0] + (0.8 / 3.0) * rho * base
    for n, ((a, b), c) in enumerate(zip(PAIRS, along(v))):
        scale = rho_axis if n < 3 else rho_edge
        even = scale * (base + 4.5 * c * c)
        odd = scale * (3.0 * c)
        out[a] = 0.2 * f[a] + (even + odd)
        out[b] = 0.2 * f[b] + (even - odd)
    return out


def collide_back(g, m, v, s):
    p = [g[a] + g[b] for a, b in PAIRS]
    d = [g[a] - g[b] for a, b in PAIRS]
    g1 = [AXIS_W * a + EDGE_W * b for a, b in moments(d)]
    xy, xz, yz = p[3] + p[4], p[5] + p[6], p[7] + p[8]
    g0 = (1.0 / 3.0) * g[0] + AXIS_W * (p[0] + p[1] + p[2]) + EDGE_W * (xy + xz + yz)
    gxx = AXIS_W * p[0] + EDGE_W * (xy + xz)
    gyy = AXIS_W * p[1] + EDGE_W * (xy + yz)
    gzz = AXIS_W * p[2] + EDGE_W * (xz + yz)
    gxy = EDGE_W * (p[3] - p[4])
    gxz = EDGE_W * (p[5] - p[6])
    gyz = EDGE_W * (p[7] - p[8])
    h = (
        gxx * v[0] + gxy * v[1] + gxz * v[2],
        gxy * v[0] + gyy * v[1] + gyz * v[2],
        gxz * v[0] + gyz * v[1] + gzz * v[2],
    )
    square = v[0] * v[0] + v[1] * v[1] + v[2] * v[2]
    b = [3.0 * g1[i] + 9.0 * h[i] - 3.0 * (g0 * v[i]) for i in range(3)]
    rest = g0 * (1.0 + 1.5 * square) - 4.5 * (v[0] * h[0] + v[1] * h[1] + v[2] * h[2])
    base = 0.8 * rest
    scale = 0.8 * s
    out = [None] * Q
    out[0] = 0.2 * g[0] + base
    for (a, o), c in zip(PAIRS, along([scale * c for c in b])):
        out[a] = 0.2 * g[a] + (base + c)
        out[o] = 0.2 * g[o] + (base - c)
    solid_bar = -0.8 * (b[0] * m[0] + b[1] * m[1] + b[2] * m[2])
    return out, solid_bar


def each_chunk(layers, rows, step_rows, body, first=0):
    chunks = rows // step_rows

    def step(i, carry):
        body(first + lax.div(i, chunks), pl.ds(pl.multiple_of(lax.rem(i, chunks) * step_rows, step_rows), step_rows))
        return carry

    lax.fori_loop(0, layers * chunks, step, 0)


def forward_kernel(
    f_hbm, cot_hbm, por_hbm, ids_hbm, slot_hbm,
    a_ref, s_ref, v_ref, m_ref, sb_ref, ids_ref, slot_ref,
    f_ref, cot_ref, por_ref, b_ref, c_ref,
    xs1, xr1, ys1, yr1, cs1, cr1, xs2, xr2, ys2, yr2, cs2, cr2, load_sem, layer_sem, send_sem, recv_sem,
):
    layers, rows, cols = f_ref.shape[1:]
    n_x, n_y = lax.axis_size("gx"), lax.axis_size("gy")
    my_x, my_y = lax.axis_index("gx"), lax.axis_index("gy")

    def device(dx, dy):
        return (lax.rem(my_x + dx + n_x, n_x), lax.rem(my_y + dy + n_y, n_y))

    straight = ((1, 0), (-1, 0), (0, 1), (0, -1))
    corners = ((1, 1), (1, -1), (-1, 1), (-1, -1))
    barrier = pltpu.get_barrier_semaphore()
    loads = [
        pltpu.make_async_copy(src, dst, load_sem.at[n])
        for n, (src, dst) in enumerate(
            ((por_hbm, por_ref), (ids_hbm, ids_ref), (slot_hbm, slot_ref), (cot_hbm, cot_ref))
        )
    ]
    layer_loads = [
        pltpu.make_async_copy(f_hbm.at[:, z], f_ref.at[:, z], layer_sem.at[z]) for z in range(layers)
    ]
    for copy in loads + layer_loads:
        copy.start()
    for dx, dy in straight + corners:
        pl.semaphore_signal(barrier, inc=1, device_id=device(dx, dy), device_id_type=MESH)

    lane = lax.broadcasted_iota(jnp.int32, (rows, cols), 1)
    lane1 = lax.broadcasted_iota(jnp.int32, (1, cols), 1)

    def copies(phase, xs, xr, ys, yr, cs, cr):
        out = []
        for n, (dx, dy) in enumerate(straight + corners):
            if n < 2:
                src, dst = xs.at[n], xr.at[n]
            elif n < 4:
                src, dst = ys.at[n - 2], yr.at[n - 2]
            else:
                src, dst = cs.at[n - 4], cr.at[n - 4]
            out.append(
                pltpu.make_async_remote_copy(
                    src_ref=src, dst_ref=dst,
                    send_sem=send_sem.at[phase, n], recv_sem=recv_sem.at[phase, n],
                    device_id=device(dx, dy), device_id_type=MESH,
                )
            )
        return out

    def pack(read, sign, kind, ys, cs, carry):
        def layer(z, carry):
            carry = list(carry)
            for q in range(Q):
                dx, dy = sign * EX[q], sign * EY[q]
                if not dx and not dy:
                    continue
                plane = read(q, z)
                if dx:
                    j = kind * 5 * layers + rank_among(q, EX) * layers + z
                    start = cols - 1 if dx > 0 else 0
                    moved = pltpu.roll(plane, lax.rem(j - start + cols, cols), 1)
                    carry[side(dx)] = jnp.where(lane == j, moved, carry[side(dx)])
                if dy:
                    jy = kind * 5 * layers + rank_among(q, EY) * layers + z
                    edge = plane[rows - 8 :] if dy > 0 else plane[:8]
                    if dx:
                        edge = pltpu.roll(edge, dx % cols, 1)
                    edge = edge[7:8] if dy > 0 else edge[0:1]
                    ys[side(dy), pl.ds(jy, 1), :] = edge
                    if dx:
                        cs[2 * side(dx) + side(dy), pl.ds(kind * layers + z, 1), :] = edge
            return tuple(carry)

        return lax.fori_loop(0, layers, layer, carry)

    def stream(read, sign, out):
        def layer(z, carry):
            for q in range(Q):
                dx, dy, dz = sign * EX[q], sign * EY[q], sign * EZ[q]
                plane = read(q, lax.rem(z - dz + layers, layers) if dz else z)
                if dx:
                    plane = pltpu.roll(plane, dx % cols, 1)
                if dy:
                    plane = pltpu.roll(plane, dy % rows, 0)
                out[q, z] = plane
            return carry

        lax.fori_loop(0, layers, layer, 0)

    def edges(sign, kind, xr, yr, cr, out):
        def layer(z, carry):
            for q in range(Q):
                dx, dy, dz = sign * EX[q], sign * EY[q], sign * EZ[q]
                if not dx and not dy:
                    continue
                from_z = lax.rem(z - dz + layers, layers) if dz else z
                end = 0 if dx > 0 else cols - 1
                if dx:
                    j = kind * 5 * layers + rank_among(q, EX) * layers + from_z
                    column = pltpu.roll(xr[side(dx)], lax.rem(end - j + cols, cols), 1)
                    if dy:
                        column = pltpu.roll(column, dy % rows, 0)
                    out[q, z] = jnp.where(lane == end, column, out[q, z])
                if dy:
                    jy = kind * 5 * layers + rank_among(q, EY) * layers + from_z
                    edge = yr[side(dy), pl.ds(jy, 1), :]
                    if dx:
                        corner = cr[2 * side(dx) + side(dy), pl.ds(kind * layers + from_z, 1), :]
                        edge = jnp.where(lane1 == end, corner, edge)
                    at = 0 if dy > 0 else rows - 1
                    out[q, z, at : at + 1, :] = edge
            return carry

        lax.fori_loop(0, layers, layer, 0)

    for copy in loads[:3]:
        copy.wait()
    bricks = layers * rows
    ids = ids_ref[0]
    slots = slot_ref[0]
    listed = ids.shape[1]
    value = jnp.zeros((1, listed), jnp.float32)
    for k in range(por_ref.shape[2]):
        value = jnp.where(slots == k, por_ref[0, 0, k], value)
    hit = lax.broadcasted_iota(jnp.int32, (bricks, listed), 0) == ids
    solid = jnp.sum(jnp.where(hit, value, 0.0), axis=1, keepdims=True)
    s_ref[...] = jnp.broadcast_to(1.0 - solid, (bricks, cols)).reshape(layers, rows, cols)

    def read_c(q, z):
        return c_ref[q, z]

    def read_cot(q, z):
        return cot_ref[q, z].astype(jnp.float32)

    zero = jnp.zeros((rows, cols), jnp.float32)
    loads[3].wait()
    ends = pack(read_cot, -1, 1, ys1, cs1, (zero, zero))

    def first_collision(z, r):
        f = [f_ref[q, z, r, :] for q in range(Q)]
        rho, m, v = density_velocity(f, s_ref[z, r, :])
        for i in range(3):
            v_ref[i, z, r, :] = v[i]
            m_ref[i, z, r, :] = m[i]
        for q, value in enumerate(collide(f, rho, v)):
            c_ref[q, z, r, :] = value

    for z in range(layers):
        layer_loads[z].wait()
        each_chunk(1, rows, 16, first_collision, z)

    ends = pack(read_c, 1, 0, ys1, cs1, ends)
    xs1[0] = ends[0]
    xs1[1] = ends[1]
    pl.semaphore_wait(barrier, len(straight + corners))
    first = copies(0, xs1, xr1, ys1, yr1, cs1, cr1)
    for copy in first:
        copy.start()
    stream(read_c, 1, a_ref)
    stream(read_cot, -1, b_ref)
    for copy in first:
        copy.wait()
    edges(1, 0, xr1, yr1, cr1, a_ref)
    edges(-1, 1, xr1, yr1, cr1, b_ref)

    def second_back(z, r):
        s = s_ref[z, r, :]
        rho, m, v = density_velocity([a_ref[q, z, r, :] for q in range(Q)], s)
        back, bar = collide_back([b_ref[q, z, r, :] for q in range(Q)], m, v, s)
        sb_ref[z, r, :] = bar
        for q, value in enumerate(back):
            c_ref[q, z, r, :] = value

    each_chunk(layers, rows, 16, second_back)

    ends = pack(read_c, -1, 0, ys2, cs2, (zero, zero))
    xs2[0] = ends[0]
    xs2[1] = ends[1]
    second = copies(1, xs2, xr2, ys2, yr2, cs2, cr2)
    for copy in second:
        copy.start()
    stream(read_c, -1, a_ref)
    for copy in second:
        copy.wait()
    edges(-1, 0, xr2, yr2, cr2, a_ref)


def last_kernel(
    g_ref, s_ref, v_ref, m_ref, sb_ref, ids_ref, slot_ref, grad_hbm, pgrad_hbm,
    grad_ref, bar_ref, pgrad_ref, layer_sem, sem,
):
    layers, rows, cols = g_ref.shape[1:]
    bricks = layers * rows

    def first_back(z, r):
        v = [v_ref[i, z, r, :] for i in range(3)]
        m = [m_ref[i, z, r, :] for i in range(3)]
        back, bar = collide_back([g_ref[q, z, r, :] for q in range(Q)], m, v, s_ref[z, r, :])
        bar_ref[z, r, :] = sb_ref[z, r, :] + bar
        for q, value in enumerate(back):
            grad_ref[q, z, r, :] = value

    stores = [
        pltpu.make_async_copy(grad_ref.at[:, z], grad_hbm.at[:, z], layer_sem.at[z]) for z in range(layers)
    ]
    for z in range(layers):
        each_chunk(1, rows, 16, first_back, z)
        stores[z].start()

    ids = ids_ref[0]
    slots = slot_ref[0]
    listed = ids.shape[1]
    hit = lax.broadcasted_iota(jnp.int32, (bricks, listed), 0) == ids
    sums = jnp.sum(bar_ref[...].reshape(bricks, cols), axis=1, keepdims=True)
    brick_sum = jnp.sum(jnp.where(hit, sums, 0.0), axis=0, keepdims=True)
    table = pgrad_ref.shape[2]
    slot_of_row = lax.broadcasted_iota(jnp.int32, (table, listed), 0)
    slot_sum = jnp.sum(jnp.where(slot_of_row == slots, brick_sum, 0.0), axis=1, keepdims=True)
    diagonal = lax.broadcasted_iota(jnp.int32, (table, table), 0) == lax.broadcasted_iota(
        jnp.int32, (table, table), 1
    )
    pgrad_ref[0] = jnp.sum(jnp.where(diagonal, slot_sum, 0.0), axis=0, keepdims=True)
    last = pltpu.make_async_copy(pgrad_ref, pgrad_hbm, sem)
    last.start()
    for copy in stores + [last]:
        copy.wait()


def on_device(f_start, cotangent, porosity, brick_ids, brick_slot):
    _, layers, rows, cols = f_start.shape
    vmem = pl.BlockSpec(memory_space=pltpu.VMEM)
    hbm = pl.BlockSpec(memory_space=pltpu.HBM)
    field = pltpu.VMEM((Q, layers, rows, cols), jnp.float32)

    def up8(count):
        return -(-count // 8) * 8

    halos = []
    for kinds in (2, 1):
        x = pltpu.VMEM((2, rows, cols), jnp.float32)
        y = pltpu.VMEM((2, up8(kinds * 5 * layers), cols), jnp.float32)
        c = pltpu.VMEM((4, up8(kinds * layers), cols), jnp.float32)
        halos += [x, x, y, y, c, c]

    def array(*shape):
        return jax.ShapeDtypeStruct(shape, jnp.float32)

    operands = [
        pltpu.with_memory_space_constraint(operand, pltpu.HBM)
        for operand in (f_start, cotangent, porosity, brick_ids, brick_slot)
    ]
    held = pl.pallas_call(
        forward_kernel,
        out_shape=(
            array(Q, layers, rows, cols),
            array(layers, rows, cols),
            array(3, layers, rows, cols),
            array(3, layers, rows, cols),
            array(layers, rows, cols),
            jax.ShapeDtypeStruct(brick_ids.shape, brick_ids.dtype),
            jax.ShapeDtypeStruct(brick_slot.shape, brick_slot.dtype),
        ),
        in_specs=[hbm] * 5,
        out_specs=(vmem,) * 7,
        scratch_shapes=[
            field,
            pltpu.VMEM(cotangent.shape, cotangent.dtype),
            pltpu.SMEM(porosity.shape, porosity.dtype),
            field,
            field,
        ]
        + halos
        + [
            pltpu.SemaphoreType.DMA((4,)),
            pltpu.SemaphoreType.DMA((layers,)),
            pltpu.SemaphoreType.DMA((2, 8)),
            pltpu.SemaphoreType.DMA((2, 8)),
        ],
        compiler_params=pltpu.CompilerParams(
            collective_id=0, has_side_effects=True, vmem_limit_bytes=24 * 1024 * 1024
        ),
    )(*operands)
    return pl.pallas_call(
        last_kernel,
        out_shape=(array(*f_start.shape), array(*porosity.shape)),
        in_specs=[vmem] * 7,
        out_specs=(hbm, hbm),
        scratch_shapes=[
            field,
            pltpu.VMEM((layers, rows, cols), jnp.float32),
            pltpu.VMEM(porosity.shape, jnp.float32),
            pltpu.SemaphoreType.DMA((layers,)),
            pltpu.SemaphoreType.DMA,
        ],
        compiler_params=pltpu.CompilerParams(vmem_limit_bytes=24 * 1024 * 1024),
    )(*held)


def solution(mesh):
    field = P(None, None, "gy", "gx")
    table = P("gx", "gy", None)
    return jax.shard_map(
        on_device,
        mesh=mesh,
        in_specs=(field, field, table, table, table),
        out_specs=(field, table),
        check_vma=False,
    )
```

time: 26.1 us -> 19.7 us (0.75)
  local copies, waits for them, and re-layouts: 5.87 us -> 0 us
  Pallas kernels: 19.4 us -> 18.9 us
    unnamed x12 -> x0, local copies, waits for them, and re-layouts: 5.87 us -> none
    pallas_call x1 -> x2, Pallas kernels: 19.4 us -> 18.9 us  [the longest x1 17.6 us: on_device(): pl.pallas_call(forward_kernel, out_shape=(array(Q, layers, rows, cols), a...]
where the time goes in v2:
time: 19.7 us; the launch traced here: 19.6 us
  Pallas kernels  18.9 us (96%)
  between operations  0.64 us (3%)
    pallas_call x1, Pallas kernels, on_device(): pl.pallas_call(forward_kernel, out_shape=(array(Q, layers, rows, cols), a...  17.6 us
    pallas_call x1, Pallas kernels, on_device(): pl.pallas_call(last_kernel, out_shape=(array(*f_start.shape), array(*poro...  1.36 us

profile of v2, /device:TPU:0, one launch (start us, length us, event | category | flops | bytes accessed | tf_op | source)
XLA Modules:
  0.0 19.6 jit_solution(12624041979030363252)
XLA Ops:
  0.6 17.6 %shard_map.68 = (f32[19,4,32,128]{3,2,1,0:T(8,128)S(1)}, f32[4,32,128]{2,1,0:T(8,128)S(1)}, f32[3,4,32,128]{3,2,1,0:T(8,128)S(1)}, f32[3,4,32,128]{3,2,1,0:T(8,1...) custom-call(f32[19,4,32,128]{3,2,1,0:T(8,128)} %f_hbm.1, ...), custom_call_target="tpu_custom_call" | custom-call | tf_op jit(solution)/shard_map/pallas_call | solution.py:360
  18.2 1.4 %shard_map.69 = (f32[19,4,32,128]{3,2,1,0:T(8,128)}, f32[1,1,16]{2,1,0:T(1,128)}) custom-call(f32[19,4,32,128]{3,2,1,0:T(8,128)S(1)} %get-tuple-element.9.g_ref, f32[4,32,128]{2,1,0:T(8,128)S(1)} %get-tuple-element.10.s_ref, f32[3,4,32,128]{3,2,1,0:T(8,128)S(1)} %get-tuple-element.11.v_ref, f32[3,4,32,128]{3,2,1,0:T(8,128)S(1)} %get-tuple-element.12.m_ref, ...), custom_call_target="tpu_custom_call" | custom-call | tf_op jit(solution)/shard_map/pallas_call | solution.py:391

commit v3 on v2

--- a/solution.py
+++ b/solution.py
@@ -153,7 +153,7 @@
                     device_id=device(dx, dy), device_id_type=MESH,
                 )
             )
-        return out
+        return out[4:] + out[:4]
 
     def pack(read, sign, kind, ys, cs, carry):
         def layer(z, carry):
@@ -179,7 +179,7 @@
                         cs[2 * side(dx) + side(dy), pl.ds(kind * layers + z, 1), :] = edge
             return tuple(carry)
 
-        return lax.fori_loop(0, layers, layer, carry)
+        return lax.fori_loop(0, layers, layer, carry, unroll=True)
 
     def stream(read, sign, out):
         def layer(z, carry):
@@ -193,14 +193,13 @@
                 out[q, z] = plane
             return carry
 
-        lax.fori_loop(0, layers, layer, 0)
+        lax.fori_loop(0, layers, layer, 0, unroll=True)
 
     def edges(sign, kind, xr, yr, cr, out):
         def layer(z, carry):
+            planes, lines = [], []
             for q in range(Q):
                 dx, dy, dz = sign * EX[q], sign * EY[q], sign * EZ[q]
-                if not dx and not dy:
-                    continue
                 from_z = lax.rem(z - dz + layers, layers) if dz else z
                 end = 0 if dx > 0 else cols - 1
                 if dx:
@@ -208,18 +207,21 @@
                     column = pltpu.roll(xr[side(dx)], lax.rem(end - j + cols, cols), 1)
                     if dy:
                         column = pltpu.roll(column, dy % rows, 0)
-                    out[q, z] = jnp.where(lane == end, column, out[q, z])
+                    planes.append((q, jnp.where(lane == end, column, out[q, z])))
                 if dy:
                     jy = kind * 5 * layers + rank_among(q, EY) * layers + from_z
-                    edge = yr[side(dy), pl.ds(jy, 1), :]
+                    line = yr[side(dy), pl.ds(jy, 1), :]
                     if dx:
                         corner = cr[2 * side(dx) + side(dy), pl.ds(kind * layers + from_z, 1), :]
-                        edge = jnp.where(lane1 == end, corner, edge)
-                    at = 0 if dy > 0 else rows - 1
-                    out[q, z, at : at + 1, :] = edge
+                        line = jnp.where(lane1 == end, corner, line)
+                    lines.append((q, 0 if dy > 0 else rows - 1, line))
+            for q, plane in planes:
+                out[q, z] = plane
+            for q, at, line in lines:
+                out[q, z, at : at + 1, :] = line
             return carry
 
-        lax.fori_loop(0, layers, layer, 0)
+        lax.fori_loop(0, layers, layer, 0, unroll=True)
 
     for copy in loads[:3]:
         copy.wait()

time: 19.7 us -> 18.5 us (0.939)
  Pallas kernels: 18.9 us -> 17.7 us
    pallas_call x1, Pallas kernels: 17.6 us -> 16.4 us  [on_device(): pl.pallas_call(forward_kernel, out_shape=(array(Q, layers, rows, cols), a...]
where the time goes in v3:
time: 18.5 us; the launch traced here: 18.4 us
  Pallas kernels  17.7 us (96%)
  between operations  0.64 us (3%)
    pallas_call x1, Pallas kernels, on_device(): pl.pallas_call(forward_kernel, out_shape=(array(Q, layers, rows, cols), a...  16.4 us
    pallas_call x1, Pallas kernels, on_device(): pl.pallas_call(last_kernel, out_shape=(array(*f_start.shape), array(*poro...  1.36 us

profile of v3, /device:TPU:0, one launch (start us, length us, event | category | flops | bytes accessed | tf_op | source)
XLA Modules:
  0.0 18.4 jit_solution(6545970478115271275)
XLA Ops:
  0.6 16.4 %shard_map.68 = (f32[19,4,32,128]{3,2,1,0:T(8,128)S(1)}, f32[4,32,128]{2,1,0:T(8,128)S(1)}, f32[3,4,32,128]{3,2,1,0:T(8,128)S(1)}, f32[3,4,32,128]{3,2,1,0:T(8,1...) custom-call(f32[19,4,32,128]{3,2,1,0:T(8,128)} %f_hbm.1, ...), custom_call_target="tpu_custom_call" | custom-call | tf_op jit(solution)/shard_map/pallas_call | solution.py:362
  17.0 1.4 %shard_map.69 = (f32[19,4,32,128]{3,2,1,0:T(8,128)}, f32[1,1,16]{2,1,0:T(1,128)}) custom-call(f32[19,4,32,128]{3,2,1,0:T(8,128)S(1)} %get-tuple-element.9.g_ref, f32[4,32,128]{2,1,0:T(8,128)S(1)} %get-tuple-element.10.s_ref, f32[3,4,32,128]{3,2,1,0:T(8,128)S(1)} %get-tuple-element.11.v_ref, f32[3,4,32,128]{3,2,1,0:T(8,128)S(1)} %get-tuple-element.12.m_ref, ...), custom_call_target="tpu_custom_call" | custom-call | tf_op jit(solution)/shard_map/pallas_call | solution.py:393
